TPU v7x, 128 devices: a whole 4x4x4 slice. The times are simulated.
128 devices in a mesh: arc: 8 (over y, x_hi), trow: 4 (over z), tcol: 4 (over x_lo, core).
Axes of the slice: x: 4 (x_hi: 2, x_lo: 2; x = x_hi * 2 + x_lo), y: 4, z: 4, core: 2. Of those that a mesh axis runs over, the one named last changes fastest.
Arguments:
- design: bfloat16 [5120, 8192], P('arc', 'tcol'), may hold values from -0.125 to 0.125
- local_design: bfloat16 [5120, 128], P('arc'), may hold values from -0.3125 to 0.3125
- lengths: int32 [16], P('arc'), may hold values from 1 to 320, 3840 in all
- regularizer: float32 [8192], P(('arc', 'trow')), may hold values from 0.2 to 2
Outputs:
- normal: float32 [8192, 8192], P(('arc', 'trow'), 'tcol')
- panel_factor: float32 [2, 8192, 512], P(None, 'tcol')
Inputs may be any that keep to these rules, and one draw needn't show every extreme that they name: `lengths`: each arc has at least one live row; some arc is full.
All inputs are finite; a program needn't handle non-finite values. No bound on the sum of `lengths` on one device may be relied on, other than what follows from the above.
Results may differ from a plain program's by a relative error of at most 0.003.
Values may be sent and summed in bfloat16 or wider, within the bound.
A program may use at most 128 MiB of HBM per device.

v0:
```python
import jax
import jax.numpy as jnp
from jax import lax
from jax.sharding import PartitionSpec as P

PANEL = 512
PANELS = 2
ridge = 0.1


def broadcast(block, axis, holder):
    block = jnp.where(lax.axis_index(axis) == holder, block, jnp.zeros_like(block))
    return lax.psum(block, axis)


def project_arcs(design, local_design, lengths):
    arc_count = lengths.shape[0]
    row_count = design.shape[0]
    capacity = row_count // arc_count
    arc_blocks = design.reshape(arc_count, capacity, design.shape[1])
    local_half = local_design.reshape(arc_count, capacity, local_design.shape[1])
    live_rows = jnp.arange(capacity, dtype=jnp.int32)[None, :] < lengths[:, None]
    arc_blocks = jnp.where(live_rows[:, :, None], arc_blocks, jnp.zeros((), design.dtype))
    local_half = jnp.where(live_rows[:, :, None], local_half, jnp.zeros((), local_design.dtype))
    local_normal = jnp.einsum(
        "acl,acm->alm", local_half, local_half, preferred_element_type=jnp.float32
    )
    local_normal = local_normal + ridge * jnp.eye(local_half.shape[2], dtype=jnp.float32)[None]
    local_factor = jnp.linalg.cholesky(local_normal)
    local_cols = local_half.astype(jnp.float32)
    basis_rows = lax.linalg.triangular_solve(
        local_factor, jnp.transpose(local_cols, (0, 2, 1)), left_side=True, lower=True
    )
    basis_rows = basis_rows.astype(jnp.bfloat16)
    loadings = jnp.einsum(
        "alc,acw->alw", basis_rows, arc_blocks, preferred_element_type=jnp.float32
    ).astype(jnp.bfloat16)
    cleaned = arc_blocks.astype(jnp.float32) - jnp.einsum(
        "alc,alw->acw", basis_rows, loadings, preferred_element_type=jnp.float32
    )
    return cleaned.astype(jnp.bfloat16).reshape(row_count, design.shape[1])


def contract_rows(left_rows, right_rows):
    return lax.dot_general(
        left_rows, right_rows, (((0,), (0,)), ((), ())), preferred_element_type=jnp.float32
    )


def per_device(design, local_design, lengths, regularizer):
    row_count, col_width = design.shape
    tile_rows = regularizer.shape[0]
    arc_total = lax.axis_size("arc")
    trow_total = lax.axis_size("trow")
    trow_index = lax.axis_index("trow")
    row_start = (lax.axis_index("arc") * trow_total + trow_index) * tile_rows
    col_start = lax.axis_index("tcol") * col_width
    projected = project_arcs(design, local_design, lengths)
    gathered = lax.all_gather(projected, "tcol", axis=1, tiled=True)
    regrouped = gathered.reshape(row_count, arc_total, trow_total, tile_rows)
    selected = lax.dynamic_slice_in_dim(regrouped, trow_index, 1, 2).reshape(
        row_count, arc_total * tile_rows
    )
    normal_block = lax.psum_scatter(
        contract_rows(selected, projected), "arc", scatter_dimension=0, tiled=True
    )
    rows_global = row_start + jnp.arange(tile_rows, dtype=jnp.int32)
    cols_global = col_start + jnp.arange(col_width, dtype=jnp.int32)
    on_diagonal = rows_global[:, None] == cols_global[None, :]
    normal_block = normal_block + jnp.where(
        on_diagonal, regularizer[:, None], jnp.zeros((), jnp.float32)
    )
    panel_factors = []
    for panel_index in range(PANELS):
        lead_col = panel_index * PANEL
        padded_rows = jnp.pad(normal_block, ((PANEL, PANEL), (0, 0)))
        slice_start = jnp.clip(lead_col - row_start + PANEL, 0, tile_rows + PANEL)
        slice_rows = lax.dynamic_slice_in_dim(padded_rows, slice_start, PANEL, 0)
        panel_global = lead_col + jnp.arange(PANEL, dtype=jnp.int32)
        in_tile = (panel_global >= row_start) & (panel_global < row_start + tile_rows)
        own_share = jnp.where(in_tile[:, None], slice_rows, jnp.zeros((), jnp.float32))
        panel_strip = lax.psum(own_share, ("arc", "trow"))
        pivot_block, row_strip = (
            broadcast(panel_strip[:, lead_col : lead_col + PANEL], "tcol", 0),
            broadcast(normal_block[:, lead_col : lead_col + PANEL], "tcol", 0),
        )
        lower_factor = jnp.linalg.cholesky(pivot_block)
        col_factor = lax.linalg.triangular_solve(
            lower_factor, panel_strip, left_side=True, lower=True
        ).T
        row_factor = lax.linalg.triangular_solve(
            lower_factor, row_strip.T, left_side=True, lower=True
        ).T
        col_factor = jnp.where(
            cols_global[:, None] >= lead_col, col_factor, jnp.zeros((), jnp.float32)
        )
        row_factor = jnp.where(
            rows_global[:, None] >= lead_col, row_factor, jnp.zeros((), jnp.float32)
        )
        normal_block = normal_block - jnp.dot(
            row_factor, col_factor.T, precision=lax.Precision.HIGHEST
        )
        panel_factors.append(col_factor)
    return (normal_block, jnp.stack(panel_factors))


def solution(mesh):
    return jax.shard_map(
        per_device,
        mesh=mesh,
        in_specs=(P("arc", "tcol"), P("arc", None), P("arc"), P(("arc", "trow"))),
        out_specs=(P(("arc", "trow"), "tcol"), P(None, "tcol", None)),
        check_vma=False,
    )
```

profile of v0, /device:TPU:1, one launch (start us, length us, event | category | flops | bytes accessed | tf_op | source)
XLA Modules:
  0.0 1569.1 jit_solution(3386765637183662593)
XLA Ops:
  9.6 23.5 %custom-call.33 = f32[2,128,128]{2,1,0:T(8,128)S(1)} custom-call(f32[2,128,128]{2,1,0:T(8,128)S(1)} %fusion.97), custom_call_target="Cholesky" | custom-call | tf_op jit(solution)/shard_map/jit(cholesky)/cholesky | solution.py:29
  33.4 19.7 %custom-call.34 = f32[2,1,128,128]{2,3,1,0:T(8,128)S(1)} custom-call(f32[2,1,128,128]{3,2,1,0:T(8,128)S(1)} %select_bitcast_fusion), custom_call_target="InvertDiagBlocksLowerTriangular" | custom-call | tf_op jit(solution)/shard_map/triangular_solve | solution.py:31
  61.2 102.4 %all-gather.2.cloned.1.call-done = bf16[640,8192]{0,1:T(8,128)(2,1)} async-done(((bf16[640,2048]{0,1:T(8,128)(2,1)}), bf16[640,8192]{0,1:T(8,128)(2,1)}) %all-gather.2.cloned.1.call-update) | async-done | bytes 10485776 | tf_op jit(solution)/shard_map/all_gather | solution.py:59
  165.6 10.2 fusion.158
  175.9 190.4 %reduce-scatter.2.cloned.1.call-done = f32[256,2048]{0,1:T(8,128)} async-done(((f32[2048,2048]{0,1:T(8,128)}), f32[256,2048]{0,1:T(8,128)}) %reduce-scatter.2.cloned.1.call-update) | async-done | bytes 2097168 | tf_op jit(solution)/shard_map/reduce_scatter | solution.py:64
  372.1 345.6 %all-reduce.10.cloned.1.call-done = f32[512,2048]{0,1:T(8,128)} async-done(((f32[512,2048]{0,1:T(8,128)}), f32[512,2048]{0,1:T(8,128)}) %all-reduce.10.cloned.1.call-update) | async-done | bytes 4194320 | tf_op jit(solution)/shard_map/psum | solution.py:82
  720.2 71.5 %all-reduce.16.cloned.1.call-done = (f32[512,512]{0,1:T(8,128)}, f32[512,256]{1,0:T(8,128)}) async-done(((f32[512,512]{0,1:T(8,128)}, f32[512,256]{1,0:T(8,128)}), (f32[512,512]{0,1:T(8,128)}, f32[512,256]{1,0:T(8,128)})) %all-reduce.16.cloned.1.call-update) | async-done | bytes 1572880 | tf_op jit(solution)/shard_map/psum | solution.py:13
  794.7 11.7 cholesky.327
  806.6 9.8 custom-call.40
  817.1 11.7 cholesky.346
  828.8 10.2 custom-call.41
  839.7 11.7 cholesky.367
  851.5 9.8 custom-call.42
  861.9 11.7 cholesky.384
  886.6 39.3 %custom-call.43 = f32[4,128,128]{1,2,0:T(8,128)S(1)} custom-call(f32[4,128,128]{2,1,0:T(8,128)S(1)} %get-tuple-element.33), custom_call_target="InvertDiagBlocksLowerTriangular" | custom-call | tf_op jit(solution)/shard_map/triangular_solve/custom-call.9 | solution.py:91
  966.0 342.8 %all-reduce.12.cloned.1.call-done = f32[512,2048]{0,1:T(8,128)} async-done(((f32[512,2048]{0,1:T(8,128)}), f32[512,2048]{0,1:T(8,128)}) %all-reduce.12.cloned.1.call-update) | async-done | bytes 4194320 | tf_op jit(solution)/shard_map/psum | solution.py:82
  1314.6 68.2 %all-reduce.14.cloned.1.call-done = (f32[512,512]{0,1:T(8,128)}, f32[512,256]{1,0:T(8,128)}) async-done(((f32[512,512]{0,1:T(8,128)}, f32[512,256]{1,0:T(8,128)}), (f32[512,512]{0,1:T(8,128)}, f32[512,256]{1,0:T(8,128)})) %all-reduce.14.cloned.1.call-update) | async-done | bytes 1572880 | tf_op jit(solution)/shard_map/psum | solution.py:13
  1385.7 11.7 cholesky.399
  1408.1 11.7 cholesky.418
  1419.8 10.2 custom-call.46
  1430.7 11.7 cholesky.439
  1442.5 9.8 custom-call.47
  1452.9 11.7 cholesky.456
  1477.6 39.3 %custom-call.48 = f32[4,128,128]{1,2,0:T(8,128)S(1)} custom-call(f32[4,128,128]{2,1,0:T(8,128)S(1)} %get-tuple-element.35), custom_call_target="InvertDiagBlocksLowerTriangular" | custom-call | tf_op jit(solution)/shard_map/triangular_solve/custom-call.9 | solution.py:91
  (192 shorter events, 168.0 us)
Async XLA Ops:
  7.2 156.4 %all-gather.2.cloned.1.call-start = ((), (), s32[]{:S(2)}) async-start(), calls=%async_computation.1 | async-start | bytes 13107200 | tf_op jit(solution)/shard_map/all_gather | solution.py:59
  61.0 305.3 %reduce-scatter.2.cloned.1.call-start = ((), (), s32[]{:S(2)}) async-start(), calls=%async_computation.2 | async-start | bytes 18874368 | tf_op jit(solution)/shard_map/reduce_scatter | solution.py:64
  175.8 190.5 %copy-start.18 = (f32[256]{0:T(256)S(1)}, f32[256]{0:T(256)}, u32[]{:S(2)}) copy-start(f32[256]{0:T(256)} %param.12) | copy-start | bytes 3076
  175.8 542.0 %all-reduce.10.cloned.1.call-start = ((), (), s32[]{:S(2)}) async-start(), calls=%async_computation.3 | async-start | bytes 8388608 | tf_op jit(solution)/shard_map/psum | solution.py:82
  368.0 3.3 copy-start
  371.2 420.5 %all-reduce.16.cloned.1.call-start = ((), (), s32[]{:S(2)}) async-start(), calls=%async_computation.6 | async-start | bytes 3145728 | tf_op jit(solution)/shard_map/psum | solution.py:13
  720.1 588.7 %all-reduce.12.cloned.1.call-start = ((), (), s32[]{:S(2)}) async-start(), calls=%async_computation.4 | async-start | bytes 8388608 | tf_op jit(solution)/shard_map/psum | solution.py:82
  886.6 48.4 %copy-start.3 = (f32[512,512]{1,0:T(8,128)}, f32[512,512]{1,0:T(8,128)S(1)}, u32[]{:S(2)}) copy-start(f32[512,512]{1,0:T(8,128)S(1)} %get-tuple-element.206) | copy-start | bytes 3145732
  942.2 8.3 copy-start.16
  942.2 13.2 copy-start.1
  942.2 13.2 copy-start.4
  942.2 13.2 copy-start.6
  942.2 13.2 copy-start.8
  950.5 8.9 copy-start.10
  963.9 347.3 %copy-start.5 = (f32[128,2048]{0,1:T(8,128)S(1)}, f32[128,2048]{0,1:T(8,128)}, u32[]{:S(2)}) copy-start(f32[128,2048]{0,1:T(8,128)} %copy.69) | copy-start | bytes 3145732
  963.9 347.3 %copy-start.7 = (f32[128,2048]{0,1:T(8,128)S(1)}, f32[128,2048]{0,1:T(8,128)}, u32[]{:S(2)}) copy-start(f32[128,2048]{0,1:T(8,128)} %copy.70) | copy-start | bytes 3145732
  963.9 347.3 %copy-start.9 = (f32[128,2048]{0,1:T(8,128)S(1)}, f32[128,2048]{0,1:T(8,128)}, u32[]{:S(2)}) copy-start(f32[128,2048]{0,1:T(8,128)} %copy.71) | copy-start | bytes 3145732
  963.9 418.8 %all-reduce.14.cloned.1.call-start = ((), (), s32[]{:S(2)}) async-start(), calls=%async_computation.5 | async-start | bytes 3145728 | tf_op jit(solution)/shard_map/psum | solution.py:13
  1477.6 48.4 %copy-start.2 = (f32[512,512]{1,0:T(8,128)}, f32[512,512]{1,0:T(8,128)S(1)}, u32[]{:S(2)}) copy-start(f32[512,512]{1,0:T(8,128)S(1)} %get-tuple-element.205) | copy-start | bytes 3145732
  1533.2 8.1 copy-start.17
  1533.2 13.0 copy-start.11
  1533.2 13.0 copy-start.12
  1533.2 13.0 copy-start.13
  1546.2 2.5 copy-start.15
  (1 other events, 1.3 us)
Sparse Core Ops, SparseCore 0:
  61.1 102.4 all-gather.1
  175.9 190.3 reduce-scatter.1
  371.4 346.3 all-reduce.9
  721.0 70.6 all-reduce.15
  964.0 344.7 all-reduce.11
  1312.0 70.6 all-reduce.13
where the time goes:
time: 1580 us; the launch traced here: 1570 us
  waiting for transfers between devices  1120 us (71%)
  other arithmetic  314 us (20%)
  matrix products  78.7 us (5%)
  local copies, waits for them, and re-layouts  34.9 us (2%)
  between operations  20 us (1%)
    psum x2, waiting for transfers between devices, per_device(): panel_strip = lax.psum(own_share, ('arc', 'trow'))  688 us
    reduce_scatter x1, waiting for transfers between devices, per_device(): lax.psum_scatter(contract_rows(selected, projected), 'arc', scatter_dimen...  190 us
    another operation x30, other arithmetic, per_device(): lower_factor = jnp.linalg.cholesky(pivot_block)  159 us
    psum x2, waiting for transfers between devices, broadcast(): return lax.psum(block, axis)  140 us
    all_gather x1, waiting for transfers between devices, per_device(): gathered = lax.all_gather(projected, 'tcol', axis=1, tiled=True)  102 us
    another operation x5, other arithmetic, per_device(): lax.linalg.triangular_solve(lower_factor, row_strip.T, left_side=True, lo...  79.2 us
    another operation x14, matrix products, per_device(): lax.linalg.triangular_solve(lower_factor, panel_strip, left_side=True, lo...  40.7 us
  transfers between devices with their start and end apart: 6, of which 6 were waited for; matrix products, arithmetic and copies ran while one was open for 0% of the time, Pallas kernels for 0%

commit v1 on v0

--- a/solution.py
+++ b/solution.py
@@ -79,7 +79,7 @@
         panel_global = lead_col + jnp.arange(PANEL, dtype=jnp.int32)
         in_tile = (panel_global >= row_start) & (panel_global < row_start + tile_rows)
         own_share = jnp.where(in_tile[:, None], slice_rows, jnp.zeros((), jnp.float32))
-        panel_strip = lax.psum(own_share, ("arc", "trow"))
+        panel_strip = lax.psum(lax.psum(own_share, "trow"), "arc")
         pivot_block, row_strip = (
             broadcast(panel_strip[:, lead_col : lead_col + PANEL], "tcol", 0),
             broadcast(normal_block[:, lead_col : lead_col + PANEL], "tcol", 0),

time: 1580 us -> 1410 us (0.89)
  waiting for transfers between devices: 1120 us -> 948 us
    psum x2 -> x4, waiting for transfers between devices: 688 us -> 560 us  [per_device(): panel_strip = lax.psum(lax.psum(own_share, 'trow'), 'arc')]
    psum x2, waiting for transfers between devices: 140 us -> 95.3 us  [broadcast(): return lax.psum(block, axis)]
  transfers between devices with their start and end apart: 6 -> 8, of which waited for: 6 -> 8; matrix products, arithmetic and copies ran while one was open for 0% -> 0% of each run, Pallas kernels for 0% -> 0%
where the time goes in v1:
time: 1410 us; the launch traced here: 1400 us
  waiting for transfers between devices  948 us (67%)
  other arithmetic  314 us (22%)
  matrix products  78.7 us (6%)
  local copies, waits for them, and re-layouts  35.5 us (3%)
  between operations  20.3 us (1%)
    psum x4, waiting for transfers between devices, per_device(): panel_strip = lax.psum(lax.psum(own_share, 'trow'), 'arc')  560 us
    reduce_scatter x1, waiting for transfers between devices, per_device(): lax.psum_scatter(contract_rows(selected, projected), 'arc', scatter_dimen...  190 us
    another operation x30, other arithmetic, per_device(): lower_factor = jnp.linalg.cholesky(pivot_block)  159 us
    all_gather x1, waiting for transfers between devices, per_device(): gathered = lax.all_gather(projected, 'tcol', axis=1, tiled=True)  102 us
    psum x2, waiting for transfers between devices, broadcast(): return lax.psum(block, axis)  95.3 us
    another operation x5, other arithmetic, per_device(): lax.linalg.triangular_solve(lower_factor, row_strip.T, left_side=True, lo...  79.2 us
    another operation x14, matrix products, per_device(): lax.linalg.triangular_solve(lower_factor, panel_strip, left_side=True, lo...  40.7 us
  transfers between devices with their start and end apart: 8, of which 8 were waited for; matrix products, arithmetic and copies ran while one was open for 0% of the time, Pallas kernels for 0%

profile of v1, /device:TPU:1, one launch (start us, length us, event | category | flops | bytes accessed | tf_op | source)
XLA Modules:
  0.0 1397.9 jit_solution(8521776717643603738)
XLA Ops:
  9.6 23.5 %custom-call.33 = f32[2,128,128]{2,1,0:T(8,128)S(1)} custom-call(f32[2,128,128]{2,1,0:T(8,128)S(1)} %fusion.97), custom_call_target="Cholesky" | custom-call | tf_op jit(solution)/shard_map/jit(cholesky)/cholesky | solution.py:29
  33.4 19.7 %custom-call.34 = f32[2,1,128,128]{2,3,1,0:T(8,128)S(1)} custom-call(f32[2,1,128,128]{3,2,1,0:T(8,128)S(1)} %select_bitcast_fusion), custom_call_target="InvertDiagBlocksLowerTriangular" | custom-call | tf_op jit(solution)/shard_map/triangular_solve | solution.py:31
  61.2 102.4 %all-gather.2.cloned.1.call-done = bf16[640,8192]{0,1:T(8,128)(2,1)} async-done(((bf16[640,2048]{0,1:T(8,128)(2,1)}), bf16[640,8192]{0,1:T(8,128)(2,1)}) %all-gather.2.cloned.1.call-update) | async-done | bytes 10485776 | tf_op jit(solution)/shard_map/all_gather | solution.py:59
  165.6 10.2 fusion.158
  175.9 190.4 %reduce-scatter.2.cloned.1.call-done = f32[256,2048]{0,1:T(8,128)} async-done(((f32[2048,2048]{0,1:T(8,128)}), f32[256,2048]{0,1:T(8,128)}) %reduce-scatter.2.cloned.1.call-update) | async-done | bytes 2097168 | tf_op jit(solution)/shard_map/reduce_scatter | solution.py:64
  371.3 95.6 %all-reduce.12.cloned.1.call-done = f32[512,2048]{0,1:T(8,128)} async-done(((f32[512,2048]{0,1:T(8,128)}), f32[512,2048]{0,1:T(8,128)}) %all-reduce.12.cloned.1.call-update) | async-done | bytes 4194320 | tf_op jit(solution)/shard_map/psum | solution.py:82
  467.9 185.8 %all-reduce.14.cloned.1.call-done = f32[512,2048]{0,1:T(8,128)} async-done(((f32[512,2048]{0,1:T(8,128)}), f32[512,2048]{0,1:T(8,128)}) %all-reduce.14.cloned.1.call-update) | async-done | bytes 4194320 | tf_op jit(solution)/shard_map/psum | solution.py:82
  656.3 49.1 %all-reduce.22.cloned.1.call-done = (f32[512,512]{0,1:T(8,128)}, f32[512,256]{1,0:T(8,128)}) async-done(((f32[512,512]{0,1:T(8,128)}, f32[512,256]{1,0:T(8,128)}), (f32[512,512]{0,1:T(8,128)}, f32[512,256]{1,0:T(8,128)})) %all-reduce.22.cloned.1.call-update) | async-done | bytes 1572880 | tf_op jit(solution)/shard_map/psum | solution.py:13
  708.3 11.7 cholesky.327
  730.7 11.7 cholesky.346
  742.4 10.2 custom-call.41
  753.4 11.7 cholesky.367
  765.1 9.8 custom-call.42
  775.5 11.7 cholesky.384
  800.8 39.3 %custom-call.43 = f32[4,128,128]{1,2,0:T(8,128)S(1)} custom-call(f32[4,128,128]{2,1,0:T(8,128)S(1)} %get-tuple-element.33), custom_call_target="InvertDiagBlocksLowerTriangular" | custom-call | tf_op jit(solution)/shard_map/triangular_solve/custom-call.9 | solution.py:91
  878.1 93.8 %all-reduce.16.cloned.1.call-done = f32[512,2048]{0,1:T(8,128)} async-done(((f32[512,2048]{0,1:T(8,128)}), f32[512,2048]{0,1:T(8,128)}) %all-reduce.16.cloned.1.call-update) | async-done | bytes 4194320 | tf_op jit(solution)/shard_map/psum | solution.py:82
  974.0 184.9 %all-reduce.18.cloned.1.call-done = f32[512,2048]{0,1:T(8,128)} async-done(((f32[512,2048]{0,1:T(8,128)}), f32[512,2048]{0,1:T(8,128)}) %all-reduce.18.cloned.1.call-update) | async-done | bytes 4194320 | tf_op jit(solution)/shard_map/psum | solution.py:82
  1164.7 46.3 %all-reduce.20.cloned.1.call-done = (f32[512,512]{0,1:T(8,128)}, f32[512,256]{1,0:T(8,128)}) async-done(((f32[512,512]{0,1:T(8,128)}, f32[512,256]{1,0:T(8,128)}), (f32[512,512]{0,1:T(8,128)}, f32[512,256]{1,0:T(8,128)})) %all-reduce.20.cloned.1.call-update) | async-done | bytes 1572880 | tf_op jit(solution)/shard_map/psum | solution.py:13
  1214.0 11.7 cholesky.399
  1236.3 11.7 cholesky.418
  1248.1 10.2 custom-call.46
  1259.0 11.7 cholesky.439
  1281.1 11.7 cholesky.456
  1306.4 39.3 %custom-call.48 = f32[4,128,128]{1,2,0:T(8,128)S(1)} custom-call(f32[4,128,128]{2,1,0:T(8,128)S(1)} %get-tuple-element.35), custom_call_target="InvertDiagBlocksLowerTriangular" | custom-call | tf_op jit(solution)/shard_map/triangular_solve/custom-call.9 | solution.py:91
  (198 shorter events, 189.3 us)
Async XLA Ops:
  7.2 156.4 %all-gather.2.cloned.1.call-start = ((), (), s32[]{:S(2)}) async-start(), calls=%async_computation.1 | async-start | bytes 13107200 | tf_op jit(solution)/shard_map/all_gather | solution.py:59
  61.0 305.3 %reduce-scatter.2.cloned.1.call-start = ((), (), s32[]{:S(2)}) async-start(), calls=%async_computation.2 | async-start | bytes 18874368 | tf_op jit(solution)/shard_map/reduce_scatter | solution.py:64
  175.8 190.5 %copy-start.18 = (f32[256]{0:T(256)S(1)}, f32[256]{0:T(256)}, u32[]{:S(2)}) copy-start(f32[256]{0:T(256)} %param.12) | copy-start | bytes 3076
  175.8 291.1 %all-reduce.12.cloned.1.call-start = ((), (), s32[]{:S(2)}) async-start(), calls=%async_computation.3 | async-start | bytes 8388608 | tf_op jit(solution)/shard_map/psum | solution.py:82
  368.0 98.9 %copy-start = (f32[256,2048]{0,1:T(8,128)}, f32[256,2048]{0,1:T(8,128)S(1)}, u32[]{:S(2)}) copy-start(f32[256,2048]{0,1:T(8,128)S(1)} %select_add_fusion) | copy-start | bytes 6291460
  371.2 282.4 %all-reduce.14.cloned.1.call-start = ((), (), s32[]{:S(2)}) async-start(), calls=%async_computation.4 | async-start | bytes 8388608 | tf_op jit(solution)/shard_map/psum | solution.py:82
  466.9 238.4 %all-reduce.22.cloned.1.call-start = ((), (), s32[]{:S(2)}) async-start(), calls=%async_computation.8 | async-start | bytes 3145728 | tf_op jit(solution)/shard_map/psum | solution.py:13
  655.9 315.9 %all-reduce.16.cloned.1.call-start = ((), (), s32[]{:S(2)}) async-start(), calls=%async_computation.5 | async-start | bytes 8388608 | tf_op jit(solution)/shard_map/psum | solution.py:82
  800.8 48.4 %copy-start.3 = (f32[512,512]{1,0:T(8,128)}, f32[512,512]{1,0:T(8,128)S(1)}, u32[]{:S(2)}) copy-start(f32[512,512]{1,0:T(8,128)S(1)} %get-tuple-element.208) | copy-start | bytes 3145732
  856.4 8.3 copy-start.16
  856.4 13.2 copy-start.1
  856.4 13.2 copy-start.4
  856.4 13.2 copy-start.6
  856.4 13.2 copy-start.8
  864.6 8.9 copy-start.10
  878.0 280.9 %all-reduce.18.cloned.1.call-start = ((), (), s32[]{:S(2)}) async-start(), calls=%async_computation.6 | async-start | bytes 8388608 | tf_op jit(solution)/shard_map/psum | solution.py:82
  971.9 189.4 %copy-start.5 = (f32[128,2048]{0,1:T(8,128)S(1)}, f32[128,2048]{0,1:T(8,128)}, u32[]{:S(2)}) copy-start(f32[128,2048]{0,1:T(8,128)} %copy.69) | copy-start | bytes 3145732
  971.9 189.4 %copy-start.7 = (f32[128,2048]{0,1:T(8,128)S(1)}, f32[128,2048]{0,1:T(8,128)}, u32[]{:S(2)}) copy-start(f32[128,2048]{0,1:T(8,128)} %copy.70) | copy-start | bytes 3145732
  971.9 189.4 %copy-start.9 = (f32[128,2048]{0,1:T(8,128)S(1)}, f32[128,2048]{0,1:T(8,128)}, u32[]{:S(2)}) copy-start(f32[128,2048]{0,1:T(8,128)} %copy.71) | copy-start | bytes 3145732
  971.9 239.1 %all-reduce.20.cloned.1.call-start = ((), (), s32[]{:S(2)}) async-start(), calls=%async_computation.7 | async-start | bytes 3145728 | tf_op jit(solution)/shard_map/psum | solution.py:13
  1306.3 48.4 %copy-start.2 = (f32[512,512]{1,0:T(8,128)}, f32[512,512]{1,0:T(8,128)S(1)}, u32[]{:S(2)}) copy-start(f32[512,512]{1,0:T(8,128)S(1)} %get-tuple-element.207) | copy-start | bytes 3145732
  1362.0 13.0 copy-start.11
  1362.0 13.0 copy-start.12
  1362.0 13.0 copy-start.13
  (3 other events, 11.9 us)
Sparse Core Ops, SparseCore 0:
  61.1 102.4 all-gather.1
  175.9 190.3 reduce-scatter.1
  371.4 95.4 all-reduce.11
  469.3 184.2 all-reduce.13
  656.6 48.6 all-reduce.21
  878.2 93.6 all-reduce.15
  974.5 184.3 all-reduce.17
  1162.3 48.6 all-reduce.19
